TPU v7x, 32 devices: a whole 2x2x4 slice. The times are simulated.
32 devices in a mesh: cases: 2 (over y), vol: 4 (over z), ctrl: 4 (over x, core).
Axes of the slice: x: 2, y: 2, z: 4, core: 2. Of those that a mesh axis runs over, the one named last changes fastest.
Arguments:
- ctrl_coords: float32 [3, 65536], replicated, may hold values from 0 to 1536
- vol_coords: float32 [3, 524288], P(None, ('vol', 'ctrl')), may hold values from 0 to 1536
- sensitivity: float32 [3, 1048576], P(None, ('cases', 'vol', 'ctrl')), parts along dimension 1, may hold values from -0.3 to 0.3
- vol_lists: int32 [4096, 7], P(('vol', 'ctrl')), may hold values from -1 to 511, as said below
- ctrl_lists: int32 [512, 5], P(('vol', 'ctrl')), may hold values from -1 to 511, as said below
Outputs:
- solution: float32 [3, 131072], P(None, ('cases', 'vol', 'ctrl')), parts along dimension 1
- residual: float32 [3, 131072], P(None, ('cases', 'vol', 'ctrl')), parts along dimension 1
There are 2 independent parts, one for each index of `cases`. A program takes and returns all parts, laid end to end along the dimension named above; an argument that names none is the same for every part. Nothing has to cross between parts.
Inputs may be any that keep to these rules, and one draw needn't show every extreme that they name: `vol_lists`: row v lists in increasing order the consecutive control tiles that may hold a point within distance 2 of a node of volume tile v, then -1 entries; every control tile holding such a point is listed. `ctrl_lists`: row t lists in increasing order the consecutive control tiles, t among them, that may hold a point within distance 2 of a point of tile t, then -1 entries; every live entry differs from t by at most 2, and the relation is symmetric.
All inputs are finite; a program needn't handle non-finite values.
Results may differ from a plain program's by a relative error of at most 0.0003.
Values sent between devices are 32-bit elements; how exact they have to be, the bound alone decides.
A program may use at most 128 MiB of HBM per device.

v0:
```python
import functools

import jax
import jax.numpy as jnp
from jax import lax
from jax.experimental import pallas as pl
from jax.experimental.pallas import tpu as pltpu
from jax.sharding import PartitionSpec as P

TILE = 128
KN = 5
BATCH = 8
HALO = 4
kernel_weight = 0.03125
MESH = pl.DeviceIdType.MESH


def split_rows(value):
    high = value.astype(jnp.bfloat16).astype(jnp.float32)
    return jnp.concatenate([high, value - high], axis=0)


def phi_tile(columns, rows):
    high, rest = [], []
    for start in range(0, TILE, 32):
        square = None
        for axis in range(4, 7):
            gap = columns[start : start + 32, axis : axis + 1] - rows[axis : axis + 1, :]
            square = gap * gap if square is None else square + gap * gap
        ratio = square * lax.rsqrt(jnp.maximum(square, 1e-30))
        margin = jnp.maximum(1.0 - ratio, 0.0)
        twice = margin * margin
        value = twice * twice * (5.0 - 4.0 * margin)
        lead = value.astype(jnp.bfloat16)
        high.append(lead)
        rest.append((value - lead.astype(jnp.float32)).astype(jnp.bfloat16))
    return jnp.concatenate(high + rest, axis=0)


def load_kernel(lists_ref, count_ref, vol_ref, ctrl_ref, load_ref):
    load_ref[...] = jnp.zeros_like(load_ref)
    last = vol_ref.shape[0] - 1

    def step(_, state):
        tile, entry = state
        found = []
        for _ in range(BATCH):
            listed = lists_ref[tile * 8 + entry]
            more = lists_ref[tile * 8 + entry + 1] >= 0
            block = vol_ref[jnp.minimum(tile, last)]
            near = jnp.maximum(listed, 0)
            live = jnp.where(listed >= 0, 1.0, 0.0).astype(jnp.float32)
            kern = phi_tile(block.T, ctrl_ref[near])
            grads = split_rows(block * live).astype(jnp.bfloat16)
            both = jnp.concatenate([grads, grads], axis=1)
            found.append((near, jnp.dot(both, kern, preferred_element_type=jnp.float32)))
            tile, entry = jnp.where(more, tile, tile + 1), jnp.where(more, entry + 1, 0)
        for near, terms in found:
            load_ref[near + HALO] += terms[0:4] + terms[8:12]
        return tile, entry

    lax.fori_loop(0, count_ref[0], step, (jnp.int32(0), jnp.int32(0)))


def solve_kernel(
    vols, ctrls, mask_ref, load_ref, points_ref, sol_ref, res_ref,
    from_pair, to_chip, from_chip, kern, field, first_w, second_w, start_w, sums_a, sums_b,
    pair_send, pair_recv, chip_send, chip_recv, a_send, a_recv, b_send, b_recv,
):
    count = vols * ctrls
    chips = count // 2
    own = sol_ref.shape[0]
    wide = own + 2 * HALO
    vol, ctrl = lax.axis_index("vol"), lax.axis_index("ctrl")
    me = vol * ctrls + ctrl
    chip, core = me // 2, me % 2

    def device(index):
        return {"vol": index // ctrls, "ctrl": index % ctrls}

    barrier = pltpu.get_barrier_semaphore()

    def greet(step, _):
        pl.semaphore_signal(
            barrier, inc=1, device_id=device((me + step) % count), device_id_type=MESH
        )
        return 0

    lax.fori_loop(1, count, greet, 0)
    pl.semaphore_wait(barrier, count - 1)

    def slab(index):
        return pl.ds(index * own, wide)

    def pair_copy(part):
        return pltpu.make_async_remote_copy(
            src_ref=load_ref.at[slab(2 * part + 1 - core)],
            dst_ref=from_pair.at[part],
            send_sem=pair_send.at[part],
            recv_sem=pair_recv.at[part],
            device_id=device(2 * chip + 1 - core),
            device_id_type=MESH,
        )

    def chip_copy(part, slot):
        return pltpu.make_async_remote_copy(
            src_ref=to_chip.at[part],
            dst_ref=from_chip.at[slot],
            send_sem=chip_send.at[part],
            recv_sem=chip_recv.at[slot],
            device_id=device(2 * part + core),
            device_id_type=MESH,
        )

    def start_pair(step, _):
        pair_copy((chip + step) % chips).start()
        return 0

    lax.fori_loop(1, chips + 1, start_pair, 0)

    def forward(step, _):
        part = (chip + step) % chips
        pair_copy(part).wait_recv()
        to_chip[part] = load_ref[slab(2 * part + core)] + from_pair[part]
        chip_copy(part, chip).start()
        return 0

    lax.fori_loop(1, chips, forward, 0)
    pair_copy(chip).wait_recv()
    start_w[...] = load_ref[slab(me)] + from_pair[chip]

    def build(row, _):
        for entry in range(KN):
            away = 1e6 * (1.0 - mask_ref[row * 8 + entry])
            kern[row, entry * 256 : entry * 256 + 256, :] = phi_tile(
                points_ref[row + entry].T, points_ref[row + 2] + away
            )
        return 0

    lax.fori_loop(0, own + HALO, build, 0)

    def gather(step, _):
        part = (chip + step) % chips
        chip_copy(part, part).wait_recv()
        start_w[...] += from_chip[part]
        return 0

    lax.fori_loop(1, chips, gather, 0)

    def spread(source, size):
        def body(row, _):
            parts = split_rows(source[row])
            field[row] = jnp.concatenate([parts, jnp.zeros_like(parts)], axis=0).astype(jnp.bfloat16)
            return 0

        lax.fori_loop(0, size, body, 0)

    def apply(source, target, size, shift):
        spread(source, size + 4)

        def body(step, _):
            mixed = []
            for turn in range(4):
                row = step * 4 + turn
                pieces = []
                for entry in range(KN):
                    pieces += [field[row + entry]] * 2
                mixed.append(
                    jnp.dot(
                        jnp.concatenate(pieces, axis=1),
                        kern[row + shift],
                        preferred_element_type=jnp.float32,
                    )
                )
            for turn in range(4):
                row = step * 4 + turn
                target[row] = source[row + 2] + kernel_weight * (mixed[turn][0:4] + mixed[turn][4:8])
            return 0

        lax.fori_loop(0, size // 4, body, 0)

    def share(sums, send, recv):
        def copy(peer, slot):
            return pltpu.make_async_remote_copy(
                src_ref=sums.at[me],
                dst_ref=sums.at[slot],
                send_sem=send.at[peer],
                recv_sem=recv.at[slot],
                device_id=device(peer),
                device_id_type=MESH,
            )

        def begin(step, _):
            copy((me + step) % count, me).start()
            return 0

        def collect(step, total):
            peer = (me + step) % count
            copy(peer, peer).wait_recv()
            return total + sums[peer]

        def finish(step, _):
            copy((me + step) % count, me).wait_send()
            return 0

        return (
            lambda: lax.fori_loop(1, count, begin, 0),
            lambda: lax.fori_loop(1, count, collect, sums[me]),
            lambda: lax.fori_loop(1, count, finish, 0),
        )

    apply(start_w, first_w, own + 4, 0)
    r0 = start_w[HALO : HALO + own]
    w1 = first_w[2 : 2 + own]
    sums_a[me] = jnp.concatenate([jnp.sum(r0 * r0, axis=0), jnp.sum(r0 * w1, axis=0)], axis=0)
    begin_a, collect_a, finish_a = share(sums_a, a_send, a_recv)
    begin_b, collect_b, finish_b = share(sums_b, b_send, b_recv)
    begin_a()
    apply(first_w, second_w, own, 2)
    total = collect_a()
    rr0, energy0 = jnp.sum(total[0:4]), jnp.sum(total[4:8])
    alpha0 = rr0 / energy0
    r0 = start_w[HALO : HALO + own]
    w1 = first_w[2 : 2 + own]
    r1 = r0 - alpha0 * w1
    image = w1 - alpha0 * second_w[...]
    sums_b[me] = jnp.concatenate(
        [jnp.sum(r1 * r1, axis=0), jnp.sum(r1 * image, axis=0), jnp.sum(r1 * w1, axis=0), jnp.zeros((4, TILE), jnp.float32)],
        axis=0,
    )
    begin_b()
    total = collect_b()
    rr1 = jnp.sum(total[0:4])
    beta = rr1 / rr0
    energy1 = jnp.sum(total[4:8]) + 2.0 * beta * jnp.sum(total[8:12]) + beta * beta * energy0
    alpha1 = rr1 / energy1
    r0 = start_w[HALO : HALO + own]
    w1 = first_w[2 : 2 + own]
    r1 = r0 - alpha0 * w1
    sol_ref[...] = alpha0 * r0 + alpha1 * (r1 + beta * r0)
    res_ref[...] = r1 - alpha1 * (w1 - alpha0 * second_w[...] + beta * w1)

    def drain_pair(part, _):
        pair_copy(part).wait_send()
        return 0

    def drain_chip(step, _):
        chip_copy((chip + step) % chips, chip).wait_send()
        return 0

    lax.fori_loop(0, chips, drain_pair, 0)
    lax.fori_loop(1, chips, drain_chip, 0)
    finish_a()
    finish_b()


def with_neighbours(rows, axes):
    count = lax.axis_size(axes)
    pairs = [(i, i + 1) for i in range(count - 1)]
    before = lax.ppermute(rows[-2:], axes, pairs)
    after = lax.ppermute(rows[:2], axes, [(j, i) for i, j in pairs])
    return jnp.concatenate([before, rows, after], axis=0)


def body(vols, ctrls, ctrl_coords, vol_coords, sensitivity, vol_lists, ctrl_lists):
    f32 = jnp.float32
    axes = ("vol", "ctrl")
    count = vols * ctrls
    tiles = ctrl_coords.shape[1] // TILE
    own = ctrl_lists.shape[0]
    wide = own + 2 * HALO
    vol_tiles = vol_lists.shape[0]
    first = lax.axis_index(axes) * own

    ids = first + jnp.arange(own, dtype=jnp.int32)
    wanted = ids[:, None] + jnp.arange(-2, 3, dtype=jnp.int32)
    listed = jnp.any(ctrl_lists[:, :, None] == wanted[:, None, :], axis=1) & (wanted >= 0)
    mask = with_neighbours(jnp.pad(listed.astype(f32), ((0, 0), (0, 3))), axes).reshape(-1)

    halves = (0.5 * ctrl_coords).reshape(3, tiles, TILE).transpose(1, 0, 2)
    ctrl_pack = jnp.pad(halves, ((0, 0), (4, 1), (0, 0)))
    points = lax.dynamic_slice_in_dim(jnp.pad(ctrl_pack, ((HALO, HALO), (0, 0), (0, 0))), first, wide, 0)
    vol_pack = jnp.concatenate(
        [
            jnp.pad(sensitivity.reshape(3, vol_tiles, TILE), ((0, 1), (0, 0), (0, 0))),
            jnp.pad((0.5 * vol_coords).reshape(3, vol_tiles, TILE), ((0, 1), (0, 0), (0, 0))),
        ],
        axis=0,
    ).transpose(1, 0, 2)
    lists = jnp.pad(vol_lists, ((0, BATCH), (0, 8 - vol_lists.shape[1])), constant_values=-1)
    pairs = jnp.sum(jnp.maximum(jnp.sum((vol_lists >= 0).astype(jnp.int32), axis=1), 1))
    rounds = ((pairs + BATCH - 1) // BATCH).reshape(1)

    vmem = pl.BlockSpec(memory_space=pltpu.VMEM)
    smem = pl.BlockSpec(memory_space=pltpu.SMEM)
    load = pl.pallas_call(
        load_kernel,
        out_shape=jax.ShapeDtypeStruct((tiles + 2 * HALO, 4, TILE), f32),
        in_specs=[smem, smem, vmem, vmem],
        out_specs=vmem,
        compiler_params=pltpu.CompilerParams(vmem_limit_bytes=40 * 2**20),
        name="load_terms",
    )(lists.reshape(-1), rounds, vol_pack, ctrl_pack)

    chips = count // 2
    dma = pltpu.SemaphoreType.DMA
    answer = jax.ShapeDtypeStruct((own, 4, TILE), f32)
    sol, res = pl.pallas_call(
        functools.partial(solve_kernel, vols, ctrls),
        out_shape=(answer, answer),
        in_specs=[smem, vmem, vmem],
        out_specs=(vmem, vmem),
        scratch_shapes=[
            pltpu.VMEM((chips, wide, 4, TILE), f32),
            pltpu.VMEM((chips, wide, 4, TILE), f32),
            pltpu.VMEM((chips, wide, 4, TILE), f32),
            pltpu.VMEM((own + 4, KN * 256, TILE), jnp.bfloat16),
            pltpu.VMEM((wide, 16, TILE), jnp.bfloat16),
            pltpu.VMEM((own + 4, 4, TILE), f32),
            pltpu.VMEM((own, 4, TILE), f32),
            pltpu.VMEM((wide, 4, TILE), f32),
            pltpu.VMEM((count, 8, TILE), f32),
            pltpu.VMEM((count, 16, TILE), f32),
            dma((chips,)), dma((chips,)), dma((chips,)), dma((chips,)),
            dma((count,)), dma((count,)), dma((count,)), dma((count,)),
        ],
        compiler_params=pltpu.CompilerParams(
            collective_id=0, has_side_effects=True, vmem_limit_bytes=40 * 2**20
        ),
        name="scatter_and_solve",
    )(mask, load, points)

    def unpack(value):
        return value.transpose(1, 0, 2)[:3].reshape(3, own * TILE)

    return unpack(sol), unpack(res)


def solution(mesh):
    placed = (
        P(),
        P(None, ("vol", "ctrl")),
        P(None, ("cases", "vol", "ctrl")),
        P(("vol", "ctrl"), None),
        P(("vol", "ctrl"), None),
    )
    return jax.shard_map(
        functools.partial(body, mesh.shape["vol"], mesh.shape["ctrl"]),
        mesh=mesh,
        in_specs=placed,
        out_specs=(P(None, ("cases", "vol", "ctrl")), P(None, ("cases", "vol", "ctrl"))),
        check_vma=False,
    )
```

profile of v0, /device:TPU:0, one launch (start us, length us, event | category | flops | bytes accessed | tf_op | source)
XLA Modules:
  0.0 165.0 jit_solution(9289440401839453025)
XLA Ops:
  0.6 0.0 copy-start.2
  0.7 0.1 broadcast_add_fusion
  0.7 0.7 compare_reduce_fusion
  1.5 0.1 compare_and_fusion
  1.6 0.1 fusion.1
  1.6 2.3 %collective-permute-start = (f32[2,8]{0,1:T(8,128)S(1)}, f32[2,8]{0,1:T(8,128)S(1)}, u32[]{:S(2)}, u32[]{:S(2)}) collective-permute-start(f32[2,8]{0,1:T(8,128)S(1)} %get-tuple-element.6), channel_id=1, source_target_pairs={{0,1},{1,2},{2,3},{3,4},{4,5},{5,6},{6,7},{7,8},{8,9},{9,10},{10,1... | collective-permute-start | bytes 200 | tf_op jit(solution)/shard_map/ppermute | solution.py:260
  4.0 1.3 collective-permute-start.1
  5.3 0.7 convert_reduce_fusion
  6.0 0.6 maximum_reduce_fusion
  7.3 0.8 copy.16
  8.2 1.5 multiply_bitcast_fusion
  9.6 0.0 copy-done.2
  9.6 0.9 multiply_bitcast_fusion.1
  10.5 0.1 reshape.61.lists_ref
  10.7 0.0 copy-start.1
  10.7 0.2 pad.31.ctrl_ref
  10.9 0.8 copy-done.1
  11.7 2.3 %fusion.vol_ref = f32[256,8,128]{2,1,0:T(8,128)} fusion(f32[3,256,128]{2,0,1:T(4,128)S(1)} %copy-done.1, f32[3,256,128]{2,0,1:T(4,128)} %bitcast.18), kind=kLoop, calls=%fused_computation.2 | loop fusion | flops 1310720 | bytes 1835008 | tf_op jit(solution)/shard_map/transpose | solution.py:289
  14.0 0.0 copy-start
  14.0 1.2 copy-done
  15.2 90.4 %load_terms.1.load_ref = f32[520,4,128]{2,1,0:T(4,128)S(1)} custom-call(s32[2112]{0:T(1024)S(1)} %reshape.61.lists_ref, s32[1]{0:T(128)} %bitcast.count_ref, f32[256,8,128]{2,1,0:T(8,128)S(1)} %copy-done, f32[512,8,128]{2,1,0:T(8,128)S(1)} %pad.31.ctrl_ref), custom_call_target="tpu_custom_call" | custom-call | tf_op jit(solution)/shard_map/load_terms/pallas_call | solution.py:296
  105.6 0.0 collective-permute-done
  105.6 0.0 collective-permute-done.1
  105.6 0.1 pad_maximum_fusion
  105.7 0.1 copy.14
  105.8 0.1 reshape.60.mask_ref
  105.9 58.4 %scatter_and_solve.1 = (f32[32,4,128]{2,1,0:T(4,128)S(1)}, f32[32,4,128]{2,1,0:T(4,128)S(1)}) custom-call(f32[288]{0:T(512)S(1)} %reshape.60.mask_ref, f32[520,4,128]{2,1,0:T(4,128)S(1)} %load_terms.1.load_ref, f32[40,8,128]{2,1,0:T(8,128)S(1)} %pad_dynamic-slice_fusion.points_ref), custom_call_target="tpu_custom_call" | custom-call | tf_op jit(solution)/shard_map/scatter_and_solve/pallas_call | solution.py:308
  164.3 0.7 slice_bitcast_fusion
  (5 shorter events, 0.0 us)
Async XLA Ops:
  0.6 9.0 %copy-start.2 = (f32[3,32768]{1,0:T(4,128)S(1)}, f32[3,32768]{1,0:T(4,128)}, u32[]{:S(2)}) copy-start(f32[3,32768]{1,0:T(4,128)} %param.6) | copy-start | bytes 1179652
  1.6 104.0 %collective-permute-start = (f32[2,8]{0,1:T(8,128)S(1)}, f32[2,8]{0,1:T(8,128)S(1)}, u32[]{:S(2)}, u32[]{:S(2)}) collective-permute-start(f32[2,8]{0,1:T(8,128)S(1)} %get-tuple-element.6), channel_id=1, source_target_pairs={{0,1},{1,2},{2,3},{3,4},{4,5},{5,6},{6,7},{7,8},{8,9},{9,10},{10,1... | collective-permute-start | bytes 200 | tf_op jit(solution)/shard_map/ppermute | solution.py:260
  4.0 101.6 %collective-permute-start.1 = (f32[2,8]{0,1:T(8,128)S(1)}, f32[2,8]{0,1:T(8,128)S(1)}, u32[]{:S(2)}, u32[]{:S(2)}) collective-permute-start(f32[2,8]{0,1:T(8,128)S(1)} %get-tuple-element.7), channel_id=1, source_target_pairs={{1,0},{2,1},{3,2},{4,3},{5,4},{6,5},{7,6},{8,7},{9,8},{10,9},{11,1... | collective-permute-start | bytes 200 | tf_op jit(solution)/shard_map/ppermute | solution.py:261
  10.7 1.0 copy-start.1
  14.0 1.2 copy-start
where the time goes:
time: 163 us; the launch traced here: 165 us
  Pallas kernels  149 us (91%)
  other arithmetic  6.95 us (4%)
  local copies, waits for them, and re-layouts  4.13 us (3%)
  starting transfers between devices  3.64 us (2%)
    pallas_call x1, Pallas kernels, body(): pl.pallas_call(load_kernel, out_shape=jax.ShapeDtypeStruct((tiles + 2 * H...  90.4 us
    pallas_call x1, Pallas kernels, body(): pl.pallas_call(functools.partial(solve_kernel, vols, ctrls), out_shape=(a...  58.4 us
  transfers between devices with their start and end apart: 2, of which 0 were waited for; matrix products, arithmetic and copies ran while one was open for 4% of the time, Pallas kernels for 55%

commit v1 on v0

--- a/solution.py
+++ b/solution.py
@@ -9,7 +9,9 @@
 
 TILE = 128
 KN = 5
-BATCH = 8
+BATCH = 16
+GROUP = 32
+AHEAD = 6
 HALO = 4
 kernel_weight = 0.03125
 MESH = pl.DeviceIdType.MESH
@@ -24,8 +26,8 @@
     high, rest = [], []
     for start in range(0, TILE, 32):
         square = None
-        for axis in range(4, 7):
-            gap = columns[start : start + 32, axis : axis + 1] - rows[axis : axis + 1, :]
+        for axis in range(3):
+            gap = columns(axis, start, 32) - rows[4 + axis : 5 + axis, :]
             square = gap * gap if square is None else square + gap * gap
         ratio = square * lax.rsqrt(jnp.maximum(square, 1e-30))
         margin = jnp.maximum(1.0 - ratio, 0.0)
@@ -37,34 +39,67 @@
     return jnp.concatenate(high + rest, axis=0)
 
 
-def load_kernel(lists_ref, count_ref, vol_ref, ctrl_ref, load_ref):
+def turn_columns(cols_ref, slot, block):
+    for axis in range(3):
+        row = block[4 + axis : 5 + axis, :]
+        cols_ref[slot, axis] = jnp.broadcast_to(row, (TILE, TILE)).T
+
+
+def column_reader(cols_ref, slot):
+    return lambda axis, start, size: cols_ref[slot, axis, start : start + size, :]
+
+
+def load_kernel(lists_ref, trips_ref, vol_ref, ctrl_ref, load_ref, cols_even, cols_odd):
     load_ref[...] = jnp.zeros_like(load_ref)
-    last = vol_ref.shape[0] - 1
-
-    def step(_, state):
-        tile, entry = state
-        found = []
-        for _ in range(BATCH):
-            listed = lists_ref[tile * 8 + entry]
-            more = lists_ref[tile * 8 + entry + 1] >= 0
-            block = vol_ref[jnp.minimum(tile, last)]
-            near = jnp.maximum(listed, 0)
-            live = jnp.where(listed >= 0, 1.0, 0.0).astype(jnp.float32)
-            kern = phi_tile(block.T, ctrl_ref[near])
-            grads = split_rows(block * live).astype(jnp.bfloat16)
-            both = jnp.concatenate([grads, grads], axis=1)
-            found.append((near, jnp.dot(both, kern, preferred_element_type=jnp.float32)))
-            tile, entry = jnp.where(more, tile, tile + 1), jnp.where(more, entry + 1, 0)
-        for near, terms in found:
-            load_ref[near + HALO] += terms[0:4] + terms[8:12]
-        return tile, entry
-
-    lax.fori_loop(0, count_ref[0], step, (jnp.int32(0), jnp.int32(0)))
+    groups = vol_ref.shape[0] // GROUP
+
+    def fill(slot, _):
+        turn_columns(cols_even, slot, vol_ref[slot])
+        return 0
+
+    lax.fori_loop(0, GROUP, fill, 0)
+
+    def visit(group, now, later):
+        begin = group * GROUP
+        end = begin + GROUP
+        following = jnp.minimum(group + 1, groups - 1) * GROUP
+
+        def step(index, state):
+            tile, entry = state
+            for ahead in range(AHEAD):
+                slot = jnp.minimum(index * AHEAD + ahead, GROUP - 1)
+                turn_columns(later, slot, vol_ref[following + slot])
+            found = []
+            for _ in range(BATCH):
+                inside = tile < end
+                mine = jnp.minimum(tile, end - 1)
+                listed = lists_ref[mine * 8 + entry]
+                more = lists_ref[mine * 8 + entry + 1] >= 0
+                near = jnp.maximum(listed, 0)
+                live = jnp.where(inside & (listed >= 0), 1.0, 0.0).astype(jnp.float32)
+                kern = phi_tile(column_reader(now, mine - begin), ctrl_ref[near])
+                grads = split_rows(vol_ref[mine] * live).astype(jnp.bfloat16)
+                both = jnp.concatenate([grads, grads], axis=1)
+                found.append((near, jnp.dot(both, kern, preferred_element_type=jnp.float32)))
+                tile = jnp.where(inside & jnp.logical_not(more), tile + 1, tile)
+                entry = jnp.where(inside & more, entry + 1, 0)
+            for near, terms in found:
+                load_ref[near + HALO] += terms[0:4] + terms[8:12]
+            return tile, entry
+
+        lax.fori_loop(0, trips_ref[group], step, (begin, jnp.int32(0)))
+
+    def two(index, _):
+        visit(2 * index, cols_even, cols_odd)
+        visit(2 * index + 1, cols_odd, cols_even)
+        return 0
+
+    lax.fori_loop(0, groups // 2, two, 0)
 
 
 def solve_kernel(
     vols, ctrls, mask_ref, load_ref, points_ref, sol_ref, res_ref,
-    from_pair, to_chip, from_chip, kern, field, first_w, second_w, start_w, sums_a, sums_b,
+    from_pair, to_chip, from_chip, cols, kern, field, first_w, second_w, start_w, sums_a, sums_b,
     pair_send, pair_recv, chip_send, chip_recv, a_send, a_recv, b_send, b_recv,
 ):
     count = vols * ctrls
@@ -129,11 +164,17 @@
     pair_copy(chip).wait_recv()
     start_w[...] = load_ref[slab(me)] + from_pair[chip]
 
+    def turn(row, _):
+        turn_columns(cols, row, points_ref[row])
+        return 0
+
+    lax.fori_loop(0, wide, turn, 0)
+
     def build(row, _):
         for entry in range(KN):
             away = 1e6 * (1.0 - mask_ref[row * 8 + entry])
             kern[row, entry * 256 : entry * 256 + 256, :] = phi_tile(
-                points_ref[row + entry].T, points_ref[row + 2] + away
+                column_reader(cols, row + entry), points_ref[row + 2] + away
             )
         return 0
 
@@ -287,9 +328,10 @@
         ],
         axis=0,
     ).transpose(1, 0, 2)
-    lists = jnp.pad(vol_lists, ((0, BATCH), (0, 8 - vol_lists.shape[1])), constant_values=-1)
-    pairs = jnp.sum(jnp.maximum(jnp.sum((vol_lists >= 0).astype(jnp.int32), axis=1), 1))
-    rounds = ((pairs + BATCH - 1) // BATCH).reshape(1)
+    lists = jnp.pad(vol_lists, ((0, 0), (0, 8 - vol_lists.shape[1])), constant_values=-1)
+    pairs = jnp.maximum(jnp.sum((vol_lists >= 0).astype(jnp.int32), axis=1), 1)
+    trips = (jnp.sum(pairs.reshape(-1, GROUP), axis=1) + BATCH - 1) // BATCH
+    trips = jnp.maximum(trips, -(-GROUP // AHEAD))
 
     vmem = pl.BlockSpec(memory_space=pltpu.VMEM)
     smem = pl.BlockSpec(memory_space=pltpu.SMEM)
@@ -298,9 +340,10 @@
         out_shape=jax.ShapeDtypeStruct((tiles + 2 * HALO, 4, TILE), f32),
         in_specs=[smem, smem, vmem, vmem],
         out_specs=vmem,
+        scratch_shapes=[pltpu.VMEM((GROUP, 3, TILE, TILE), f32)] * 2,
         compiler_params=pltpu.CompilerParams(vmem_limit_bytes=40 * 2**20),
         name="load_terms",
-    )(lists.reshape(-1), rounds, vol_pack, ctrl_pack)
+    )(lists.reshape(-1), trips, vol_pack, ctrl_pack)
 
     chips = count // 2
     dma = pltpu.SemaphoreType.DMA
@@ -314,6 +357,7 @@
             pltpu.VMEM((chips, wide, 4, TILE), f32),
             pltpu.VMEM((chips, wide, 4, TILE), f32),
             pltpu.VMEM((chips, wide, 4, TILE), f32),
+            pltpu.VMEM((wide, 3, TILE, TILE), f32),
             pltpu.VMEM((own + 4, KN * 256, TILE), jnp.bfloat16),
             pltpu.VMEM((wide, 16, TILE), jnp.bfloat16),
             pltpu.VMEM((own + 4, 4, TILE), f32),

time: 163 us -> 106 us (0.65); the launches traced: 165 us -> 106 us
  Pallas kernels: 149 us -> 96 us
  other arithmetic: 6.95 us -> 3.51 us
  local copies, waits for them, and re-layouts: 4.13 us -> 2.19 us
    pallas_call x1, Pallas kernels: 90.4 us -> 48.6 us  [body(): pl.pallas_call(load_kernel, out_shape=jax.ShapeDtypeStruct((tiles + 2 * H...]
    pallas_call x1, Pallas kernels: 58.4 us -> 47.4 us  [body(): pl.pallas_call(functools.partial(solve_kernel, vols, ctrls), out_shape=(a...]
    transpose x1, other arithmetic: 2.27 us -> 0.24 us  [body(): vol_pack = jnp.concatenate([jnp.pad(sensitivity.reshape(3, vol_tiles, TIL...]
    unnamed x7 -> x5, local copies, waits for them, and re-layouts: 2.85 us -> 0.83 us
  transfers between devices with their start and end apart: 2 -> 2, of which waited for: 0 -> 0; matrix products, arithmetic and copies ran while one was open for 4% -> 4% of each run, Pallas kernels for 55% -> 46%
where the time goes in v1:
time: 106 us
  Pallas kernels  96 us (91%)
  starting transfers between devices  3.64 us (3%)
  other arithmetic  3.51 us (3%)
  local copies, waits for them, and re-layouts  2.19 us (2%)
    pallas_call x1, Pallas kernels, body(): pl.pallas_call(load_kernel, out_shape=jax.ShapeDtypeStruct((tiles + 2 * H...  48.6 us
    pallas_call x1, Pallas kernels, body(): pl.pallas_call(functools.partial(solve_kernel, vols, ctrls), out_shape=(a...  47.4 us
    ppermute x1, starting transfers between devices, with_neighbours(): before = lax.ppermute(rows[-2:], axes, pairs)  2.34 us
  transfers between devices with their start and end apart: 2, of which 0 were waited for; matrix products, arithmetic and copies ran while one was open for 4% of the time, Pallas kernels for 46%

profile of v1, /device:TPU:0, one launch (start us, length us, event | category | flops | bytes accessed | tf_op | source)
XLA Modules:
  0.0 106.1 jit_solution(6578356307255079177)
XLA Ops:
  0.6 0.0 copy-start
  0.6 0.0 copy-start.1
  0.7 0.1 broadcast_add_fusion
  0.8 0.8 compare_reduce_fusion
  1.5 0.1 compare_and_fusion
  1.6 0.1 fusion.2
  1.7 2.3 %collective-permute-start = (f32[2,8]{0,1:T(8,128)S(1)}, f32[2,8]{0,1:T(8,128)S(1)}, u32[]{:S(2)}, u32[]{:S(2)}) collective-permute-start(f32[2,8]{0,1:T(8,128)S(1)} %get-tuple-element.6), channel_id=1, source_target_pairs={{0,1},{1,2},{2,3},{3,4},{4,5},{5,6},{6,7},{7,8},{8,9},{9,10},{10,1... | collective-permute-start | bytes 200 | tf_op jit(solution)/shard_map/ppermute | solution.py:301
  4.1 1.3 %collective-permute-start.1 = (f32[2,8]{0,1:T(8,128)S(1)}, f32[2,8]{0,1:T(8,128)S(1)}, u32[]{:S(2)}, u32[]{:S(2)}) collective-permute-start(f32[2,8]{0,1:T(8,128)S(1)} %get-tuple-element.7), channel_id=1, source_target_pairs={{1,0},{2,1},{3,2},{4,3},{5,4},{6,5},{7,6},{8,7},{9,8},{10,9},{11,1... | collective-permute-start | bytes 200 | tf_op jit(solution)/shard_map/ppermute | solution.py:302
  5.4 0.7 convert_reduce_fusion
  6.1 0.8 copy.16
  6.9 0.1 max.15
  7.0 0.1 reduce_sum.19
  7.1 0.1 reshape.62.lists_ref
  7.3 1.2 %multiply_bitcast_fusion.1 = f32[3,256,128]{2,0,1:T(4,128)S(1)} fusion(f32[3,32768]{1,0:T(4,128)} %param.6), kind=kLoop, calls=%fused_computation.6 | loop fusion | flops 98304 | bytes 786432 | tf_op jit(solution)/shard_map/reshape | solution.py:327
  8.4 0.0 copy-done
  8.4 0.2 multiply_bitcast_fusion
  8.7 0.0 copy-done.1
  8.7 0.2 fusion.vol_ref
  8.9 0.2 pad.31.ctrl_ref
  9.2 48.6 %load_terms.1.load_ref = f32[520,4,128]{2,1,0:T(4,128)S(1)} custom-call(s32[2048]{0:T(1024)S(1)} %reshape.62.lists_ref, s32[8]{0:T(128)S(1)} %fusion.1.trips_ref, f32[256,8,128]{2,1,0:T(8,128)S(1)} %fusion.vol_ref, f32[512,8,128]{2,1,0:T(8,128)S(1)} %pad.31.ctrl_ref), custom_call_target="tpu_custom_call" | custom-call | tf_op jit(solution)/shard_map/load_terms/pallas_call | solution.py:338
  57.8 0.0 collective-permute-done
  57.8 0.0 collective-permute-done.1
  57.8 0.1 pad_maximum_fusion
  57.8 0.1 copy.14
  57.9 0.1 reshape.61.mask_ref
  58.0 47.4 %scatter_and_solve.1 = (f32[32,4,128]{2,1,0:T(4,128)S(1)}, f32[32,4,128]{2,1,0:T(4,128)S(1)}) custom-call(f32[288]{0:T(512)S(1)} %reshape.61.mask_ref, f32[520,4,128]{2,1,0:T(4,128)S(1)} %load_terms.1.load_ref, f32[40,8,128]{2,1,0:T(8,128)S(1)} %pad_dynamic-slice_fusion.points_ref), custom_call_target="tpu_custom_call" | custom-call | tf_op jit(solution)/shard_map/scatter_and_solve/pallas_call | solution.py:351
  105.5 0.7 slice_bitcast_fusion
  (7 shorter events, 0.1 us)
Async XLA Ops:
  0.6 7.8 %copy-start = (f32[3,65536]{1,0:T(4,128)S(1)}, f32[3,65536]{1,0:T(4,128)}, u32[]{:S(2)}) copy-start(f32[3,65536]{1,0:T(4,128)} %param.5) | copy-start | bytes 2359300
  0.6 8.0 %copy-start.1 = (f32[3,32768]{1,0:T(4,128)S(1)}, f32[3,32768]{1,0:T(4,128)}, u32[]{:S(2)}) copy-start(f32[3,32768]{1,0:T(4,128)} %param.7) | copy-start | bytes 1179652
  1.7 56.0 %collective-permute-start = (f32[2,8]{0,1:T(8,128)S(1)}, f32[2,8]{0,1:T(8,128)S(1)}, u32[]{:S(2)}, u32[]{:S(2)}) collective-permute-start(f32[2,8]{0,1:T(8,128)S(1)} %get-tuple-element.6), channel_id=1, source_target_pairs={{0,1},{1,2},{2,3},{3,4},{4,5},{5,6},{6,7},{7,8},{8,9},{9,10},{10,1... | collective-permute-start | bytes 200 | tf_op jit(solution)/shard_map/ppermute | solution.py:301
  4.1 53.7 %collective-permute-start.1 = (f32[2,8]{0,1:T(8,128)S(1)}, f32[2,8]{0,1:T(8,128)S(1)}, u32[]{:S(2)}, u32[]{:S(2)}) collective-permute-start(f32[2,8]{0,1:T(8,128)S(1)} %get-tuple-element.7), channel_id=1, source_target_pairs={{1,0},{2,1},{3,2},{4,3},{5,4},{6,5},{7,6},{8,7},{9,8},{10,9},{11,1... | collective-permute-start | bytes 200 | tf_op jit(solution)/shard_map/ppermute | solution.py:302

commit v2 on v1

--- a/solution.py
+++ b/solution.py
@@ -30,9 +30,9 @@
             gap = columns(axis, start, 32) - rows[4 + axis : 5 + axis, :]
             square = gap * gap if square is None else square + gap * gap
         ratio = square * lax.rsqrt(jnp.maximum(square, 1e-30))
-        margin = jnp.maximum(1.0 - ratio, 0.0)
+        margin = jnp.maximum(4.0 - ratio, 0.0)
         twice = margin * margin
-        value = twice * twice * (5.0 - 4.0 * margin)
+        value = twice * twice * (5.0 - margin)
         lead = value.astype(jnp.bfloat16)
         high.append(lead)
         rest.append((value - lead.astype(jnp.float32)).astype(jnp.bfloat16))
@@ -49,42 +49,47 @@
     return lambda axis, start, size: cols_ref[slot, axis, start : start + size, :]
 
 
-def load_kernel(lists_ref, trips_ref, vol_ref, ctrl_ref, load_ref, cols_even, cols_odd):
+def load_kernel(
+    own, half, lists_ref, order_ref, trips_ref, grads_ref, points_ref, ctrl_ref, load_ref, cols_even, cols_odd
+):
     load_ref[...] = jnp.zeros_like(load_ref)
-    groups = vol_ref.shape[0] // GROUP
+    groups = points_ref.shape[0] // GROUP
+    active = trips_ref[groups]
 
     def fill(slot, _):
-        turn_columns(cols_even, slot, vol_ref[slot])
+        turn_columns(cols_even, slot, points_ref[order_ref[slot]])
         return 0
 
     lax.fori_loop(0, GROUP, fill, 0)
 
     def visit(group, now, later):
         begin = group * GROUP
-        end = begin + GROUP
+        end = jnp.minimum(begin + GROUP, active)
         following = jnp.minimum(group + 1, groups - 1) * GROUP
 
         def step(index, state):
             tile, entry = state
             for ahead in range(AHEAD):
                 slot = jnp.minimum(index * AHEAD + ahead, GROUP - 1)
-                turn_columns(later, slot, vol_ref[following + slot])
+                turn_columns(later, slot, points_ref[order_ref[following + slot]])
             found = []
             for _ in range(BATCH):
                 inside = tile < end
-                mine = jnp.minimum(tile, end - 1)
-                listed = lists_ref[mine * 8 + entry]
-                more = lists_ref[mine * 8 + entry + 1] >= 0
+                mine = jnp.maximum(jnp.minimum(tile, end - 1), begin)
+                real = order_ref[mine]
+                listed = lists_ref[real * 8 + entry]
+                more = lists_ref[real * 8 + entry + 1] >= 0
                 near = jnp.maximum(listed, 0)
-                live = jnp.where(inside & (listed >= 0), 1.0, 0.0).astype(jnp.float32)
+                live = jnp.where(inside & (listed >= 0), 1.0 / 256.0, 0.0).astype(jnp.float32)
                 kern = phi_tile(column_reader(now, mine - begin), ctrl_ref[near])
-                grads = split_rows(vol_ref[mine] * live).astype(jnp.bfloat16)
+                grads = split_rows(grads_ref[real] * live).astype(jnp.bfloat16)
                 both = jnp.concatenate([grads, grads], axis=1)
-                found.append((near, jnp.dot(both, kern, preferred_element_type=jnp.float32)))
+                place = lax.div(near, own) * half + lax.rem(near, half) + HALO
+                found.append((place, jnp.dot(both, kern, preferred_element_type=jnp.float32)))
                 tile = jnp.where(inside & jnp.logical_not(more), tile + 1, tile)
                 entry = jnp.where(inside & more, entry + 1, 0)
-            for near, terms in found:
-                load_ref[near + HALO] += terms[0:4] + terms[8:12]
+            for place, terms in found:
+                load_ref[place] += terms[0:8] + terms[8:16]
             return tile, entry
 
         lax.fori_loop(0, trips_ref[group], step, (begin, jnp.int32(0)))
@@ -98,9 +103,9 @@
 
 
 def solve_kernel(
-    vols, ctrls, mask_ref, load_ref, points_ref, sol_ref, res_ref,
-    from_pair, to_chip, from_chip, cols, kern, field, first_w, second_w, start_w, sums_a, sums_b,
-    pair_send, pair_recv, chip_send, chip_recv, a_send, a_recv, b_send, b_recv,
+    vols, ctrls, shared, mask_ref, load_ref, points_ref, sol_ref, res_ref,
+    from_pair, to_chip, from_chip, gathered, to_case, parts, cols, kern, field, first_w, second_w, start_w, sums_a, sums_b,
+    pair_send, pair_recv, chip_send, chip_recv, a_send, a_recv, b_send, b_recv, case_send, case_recv,
 ):
     count = vols * ctrls
     chips = count // 2
@@ -109,6 +114,9 @@
     vol, ctrl = lax.axis_index("vol"), lax.axis_index("ctrl")
     me = vol * ctrls + ctrl
     chip, core = me // 2, me % 2
+    case = lax.axis_index("cases")
+    half = own // 2 if shared else own
+    width = gathered.shape[0]
 
     def device(index):
         return {"vol": index // ctrls, "ctrl": index % ctrls}
@@ -122,10 +130,12 @@
         return 0
 
     lax.fori_loop(1, count, greet, 0)
-    pl.semaphore_wait(barrier, count - 1)
+    if shared:
+        pl.semaphore_signal(barrier, inc=1, device_id={"cases": 1 - case}, device_id_type=MESH)
+    pl.semaphore_wait(barrier, count if shared else count - 1)
 
     def slab(index):
-        return pl.ds(index * own, wide)
+        return pl.ds(index * half + (HALO - HALO * case if shared else 0), width)
 
     def pair_copy(part):
         return pltpu.make_async_remote_copy(
@@ -162,7 +172,7 @@
 
     lax.fori_loop(1, chips, forward, 0)
     pair_copy(chip).wait_recv()
-    start_w[...] = load_ref[slab(me)] + from_pair[chip]
+    gathered[...] = load_ref[slab(me)] + from_pair[chip]
 
     def turn(row, _):
         turn_columns(cols, row, points_ref[row])
@@ -183,10 +193,30 @@
     def gather(step, _):
         part = (chip + step) % chips
         chip_copy(part, part).wait_recv()
-        start_w[...] += from_chip[part]
+        gathered[...] += from_chip[part]
         return 0
 
     lax.fori_loop(1, chips, gather, 0)
+
+    if shared:
+        parts[case] = gathered[:, 0:4]
+        to_case[...] = gathered[:, 4:8]
+        swap = pltpu.make_async_remote_copy(
+            src_ref=to_case,
+            dst_ref=parts.at[case],
+            send_sem=case_send.at[0],
+            recv_sem=case_recv.at[0],
+            device_id={"cases": 1 - case},
+            device_id_type=MESH,
+        )
+        swap.start()
+        swap.wait()
+        start_w[HALO : HALO + half] = parts[0, 0:half]
+        start_w[HALO + own : wide] = parts[0, half:width]
+        start_w[0:HALO] = parts[1, 0:HALO]
+        start_w[HALO + half : HALO + own] = parts[1, HALO:width]
+    else:
+        start_w[...] = gathered[:, 0:4]
 
     def spread(source, size):
         def body(row, _):
@@ -215,7 +245,7 @@
                 )
             for turn in range(4):
                 row = step * 4 + turn
-                target[row] = source[row + 2] + kernel_weight * (mixed[turn][0:4] + mixed[turn][4:8])
+                target[row] = source[row + 2] + kernel_weight / 256.0 * (mixed[turn][0:4] + mixed[turn][4:8])
             return 0
 
         lax.fori_loop(0, size // 4, body, 0)
@@ -318,45 +348,68 @@
     listed = jnp.any(ctrl_lists[:, :, None] == wanted[:, None, :], axis=1) & (wanted >= 0)
     mask = with_neighbours(jnp.pad(listed.astype(f32), ((0, 0), (0, 3))), axes).reshape(-1)
 
-    halves = (0.5 * ctrl_coords).reshape(3, tiles, TILE).transpose(1, 0, 2)
-    ctrl_pack = jnp.pad(halves, ((0, 0), (4, 1), (0, 0)))
+    doubles = (2.0 * ctrl_coords).reshape(3, tiles, TILE).transpose(1, 0, 2)
+    ctrl_pack = jnp.pad(doubles, ((0, 0), (4, 1), (0, 0)))
     points = lax.dynamic_slice_in_dim(jnp.pad(ctrl_pack, ((HALO, HALO), (0, 0), (0, 0))), first, wide, 0)
-    vol_pack = jnp.concatenate(
-        [
-            jnp.pad(sensitivity.reshape(3, vol_tiles, TILE), ((0, 1), (0, 0), (0, 0))),
-            jnp.pad((0.5 * vol_coords).reshape(3, vol_tiles, TILE), ((0, 1), (0, 0), (0, 0))),
-        ],
-        axis=0,
-    ).transpose(1, 0, 2)
-    lists = jnp.pad(vol_lists, ((0, 0), (0, 8 - vol_lists.shape[1])), constant_values=-1)
-    pairs = jnp.maximum(jnp.sum((vol_lists >= 0).astype(jnp.int32), axis=1), 1)
-    trips = (jnp.sum(pairs.reshape(-1, GROUP), axis=1) + BATCH - 1) // BATCH
-    trips = jnp.maximum(trips, -(-GROUP // AHEAD))
+    vol_pack = jnp.pad((2.0 * vol_coords).reshape(3, vol_tiles, TILE).transpose(1, 0, 2), ((0, 0), (4, 1), (0, 0)))
+
+    shared = lax.axis_size("cases") == 2 and own % 2 == 0 and own // 2 >= HALO
+    half = own // 2 if shared else own
+    width = half + HALO if shared else wide
+    if shared:
+        other = lax.ppermute(sensitivity, "cases", [(0, 1), (1, 0)])
+        live = (vol_lists >= 0) & (vol_lists // half % 2 == lax.axis_index("cases"))
+    else:
+        other = jnp.zeros_like(sensitivity)
+        live = vol_lists >= 0
+
+    def by_tile(value):
+        return jnp.pad(value.reshape(3, vol_tiles, TILE), ((0, 1), (0, 0), (0, 0)))
+
+    grads = jnp.concatenate([by_tile(sensitivity), by_tile(other)], axis=0).transpose(1, 0, 2)
+    rank = jnp.cumsum(live.astype(jnp.int32), axis=1) - 1
+    slots = jnp.arange(8, dtype=jnp.int32)
+    chosen = live[:, :, None] & (rank[:, :, None] == slots)
+    lists = jnp.sum(jnp.where(chosen, vol_lists[:, :, None] + 1, 0), axis=1) - 1
+    pairs = jnp.sum(live.astype(jnp.int32), axis=1)
+    place = jnp.cumsum((pairs > 0).astype(jnp.int32)) - 1
+    active = place[-1] + 1
+    at = jnp.arange(vol_tiles, dtype=jnp.int32)
+    taken = (place[None, :] == at[:, None]) & (pairs > 0)[None, :]
+    order = jnp.sum(jnp.where(taken, at[None, :], 0), axis=1)
+    sizes = jnp.sum(jnp.where(taken, pairs[None, :], 0), axis=1)
+    batches = (jnp.sum(sizes.reshape(-1, GROUP), axis=1) + BATCH - 1) // BATCH
+    trips = jnp.where(batches > 0, jnp.maximum(batches, -(-GROUP // AHEAD)), 0)
+    trips = jnp.concatenate([trips, active[None]])
 
     vmem = pl.BlockSpec(memory_space=pltpu.VMEM)
     smem = pl.BlockSpec(memory_space=pltpu.SMEM)
+    load_tiles = tiles // own * half + 2 * HALO
     load = pl.pallas_call(
-        load_kernel,
-        out_shape=jax.ShapeDtypeStruct((tiles + 2 * HALO, 4, TILE), f32),
-        in_specs=[smem, smem, vmem, vmem],
+        functools.partial(load_kernel, own, half),
+        out_shape=jax.ShapeDtypeStruct((load_tiles, 8, TILE), f32),
+        in_specs=[smem, smem, smem, vmem, vmem, vmem],
         out_specs=vmem,
         scratch_shapes=[pltpu.VMEM((GROUP, 3, TILE, TILE), f32)] * 2,
         compiler_params=pltpu.CompilerParams(vmem_limit_bytes=40 * 2**20),
         name="load_terms",
-    )(lists.reshape(-1), trips, vol_pack, ctrl_pack)
+    )(lists.reshape(-1), order, trips, grads, vol_pack, ctrl_pack)
 
     chips = count // 2
     dma = pltpu.SemaphoreType.DMA
     answer = jax.ShapeDtypeStruct((own, 4, TILE), f32)
     sol, res = pl.pallas_call(
-        functools.partial(solve_kernel, vols, ctrls),
+        functools.partial(solve_kernel, vols, ctrls, shared),
         out_shape=(answer, answer),
         in_specs=[smem, vmem, vmem],
         out_specs=(vmem, vmem),
         scratch_shapes=[
-            pltpu.VMEM((chips, wide, 4, TILE), f32),
-            pltpu.VMEM((chips, wide, 4, TILE), f32),
-            pltpu.VMEM((chips, wide, 4, TILE), f32),
+            pltpu.VMEM((chips, width, 8, TILE), f32),
+            pltpu.VMEM((chips, width, 8, TILE), f32),
+            pltpu.VMEM((chips, width, 8, TILE), f32),
+            pltpu.VMEM((width, 8, TILE), f32),
+            pltpu.VMEM((width, 4, TILE), f32),
+            pltpu.VMEM((2, width, 4, TILE), f32),
             pltpu.VMEM((wide, 3, TILE, TILE), f32),
             pltpu.VMEM((own + 4, KN * 256, TILE), jnp.bfloat16),
             pltpu.VMEM((wide, 16, TILE), jnp.bfloat16),
@@ -366,7 +419,7 @@
             pltpu.VMEM((count, 8, TILE), f32),
             pltpu.VMEM((count, 16, TILE), f32),
             dma((chips,)), dma((chips,)), dma((chips,)), dma((chips,)),
-            dma((count,)), dma((count,)), dma((count,)), dma((count,)),
+            dma((count,)), dma((count,)), dma((count,)), dma((count,)), dma((1,)), dma((1,)),
         ],
         compiler_params=pltpu.CompilerParams(
             collective_id=0, has_side_effects=True, vmem_limit_bytes=40 * 2**20

time: 106 us -> 89.7 us (0.85)
  Pallas kernels: 96 us -> 71.8 us
  waiting for transfers between devices: 0.01 us -> 2.24 us
  starting transfers between devices: 3.64 us -> 5.77 us
  other arithmetic: 3.51 us -> 5.55 us
    pallas_call x2, Pallas kernels: 96 us -> 71.8 us  [the longest x1 41.5 us: body(): pl.pallas_call(functools.partial(solve_kernel, vols, ctrls, shared), out_...]
    ppermute x0 -> x1, starting transfers between devices: none -> 3.03 us  [body(): other = lax.ppermute(sensitivity, 'cases', [(0, 1), (1, 0)])]
    transpose x2 -> x3, other arithmetic: 0.47 us -> 3 us  [the longest x1 1.45 us: body(): doubles = (2.0 * ctrl_coords).reshape(3, tiles, TILE).transpose(1, 0, 2)]
    ppermute x0 -> x1, waiting for transfers between devices: none -> 2.24 us  [body(): other = lax.ppermute(sensitivity, 'cases', [(0, 1), (1, 0)])]
    reshape x1 -> x0, other arithmetic: 1.16 us -> none  [body(): (0.5 * vol_coords).reshape(3, vol_tiles, TILE)]
  transfers between devices with their start and end apart: 2 -> 3, of which waited for: 0 -> 1; matrix products, arithmetic and copies ran while one was open for 4% -> 6% of each run, Pallas kernels for 46% -> 0%
where the time goes in v2:
time: 89.7 us; the launch traced here: 89.8 us
  Pallas kernels  71.8 us (80%)
  starting transfers between devices  5.77 us (6%)
  other arithmetic  5.55 us (6%)
  local copies, waits for them, and re-layouts  3.03 us (3%)
  waiting for transfers between devices  2.24 us (2%)
  between operations  1.43 us (2%)
    pallas_call x1, Pallas kernels, body(): pl.pallas_call(functools.partial(solve_kernel, vols, ctrls, shared), out_...  41.5 us
    pallas_call x1, Pallas kernels, body(): pl.pallas_call(functools.partial(load_kernel, own, half), out_shape=jax.S...  30.3 us
    ppermute x1, starting transfers between devices, body(): other = lax.ppermute(sensitivity, 'cases', [(0, 1), (1, 0)])  3.03 us
    ppermute x1, waiting for transfers between devices, body(): other = lax.ppermute(sensitivity, 'cases', [(0, 1), (1, 0)])  2.24 us
  transfers between devices with their start and end apart: 3, of which 1 were waited for; matrix products, arithmetic and copies ran while one was open for 6% of the time, Pallas kernels for 0%

profile of v2, /device:TPU:0, one launch (start us, length us, event | category | flops | bytes accessed | tf_op | source)
XLA Modules:
  0.0 89.8 jit_solution(585416614011683979)
XLA Ops:
  0.6 3.0 %collective-permute-start.2 = (f32[3,32768]{1,0:T(4,128)}, f32[3,32768]{1,0:T(4,128)}, u32[]{:S(2)}, u32[]{:S(2)}) collective-permute-start(f32[3,32768]{1,0:T(4,128)} %param.7), channel_id=1, source_target_pairs={{0,16},{16,0},{1,17},{17,1},{2,18},{18,2},{3,19},{19,3},{4,20},{20... | collective-permute-start | bytes 1179656 | tf_op jit(solution)/shard_map/ppermute | solution.py:360
  3.7 0.1 broadcast_add_fusion.3
  3.7 0.7 compare_reduce_fusion
  4.4 0.1 compare_and_fusion
  4.5 0.1 fusion.9
  4.6 1.4 %collective-permute-start = (f32[2,8]{0,1:T(8,128)S(1)}, f32[2,8]{0,1:T(8,128)S(1)}, u32[]{:S(2)}, u32[]{:S(2)}) collective-permute-start(f32[2,8]{0,1:T(8,128)S(1)} %get-tuple-element.13), channel_id=1, source_target_pairs={{0,1},{1,2},{2,3},{3,4},{4,5},{5,6},{6,7},{7,8},{8,9},{9,10},{10,1... | collective-permute-start | bytes 200 | tf_op jit(solution)/shard_map/ppermute | solution.py:331
  6.1 1.3 %collective-permute-start.1 = (f32[2,8]{0,1:T(8,128)S(1)}, f32[2,8]{0,1:T(8,128)S(1)}, u32[]{:S(2)}, u32[]{:S(2)}) collective-permute-start(f32[2,8]{0,1:T(8,128)S(1)} %get-tuple-element.14), channel_id=1, source_target_pairs={{1,0},{2,1},{3,2},{4,3},{5,4},{6,5},{7,6},{8,7},{9,8},{10,9},{11,1... | collective-permute-start | bytes 200 | tf_op jit(solution)/shard_map/ppermute | solution.py:332
  7.4 0.7 convert_reduce_fusion
  8.1 0.3 reduce-window.9
  8.4 0.1 slice.24
  8.5 0.1 slice_reduce_fusion
  8.6 0.1 add_bitcast_fusion
  8.7 0.6 slice.26
  9.3 0.2 select_reduce_fusion
  9.5 0.1 reshape.113
  9.6 0.1 reduce_sum.49
  9.8 1.5 %multiply_bitcast_fusion = f32[512,3,128]{2,1,0:T(4,128)S(1)} fusion(f32[3,65536]{1,0:T(4,128)} %param.5), kind=kLoop, calls=%fused_computation.5 | loop fusion | flops 196608 | bytes 1572864 | tf_op jit(solution)/shard_map/transpose | solution.py:351
  11.9 0.2 pad.31.ctrl_ref
  12.1 0.0 copy-start
  12.2 0.1 pad_add_fusion.trips_ref
  12.2 0.1 copy.22
  12.4 0.1 sub.34.lists_ref
  12.5 0.7 copy-done
  13.2 0.1 multiply_bitcast_fusion.1
  13.3 0.1 pad.30.points_ref
  13.4 0.0 collective-permute-done
  13.4 0.0 collective-permute-done.1
  13.4 0.1 pad_maximum_fusion
  13.5 0.1 copy.21
  13.6 0.1 reshape.111.mask_ref
  13.7 2.2 %collective-permute-done.2 = f32[3,32768]{1,0:T(4,128)} collective-permute-done((f32[3,32768]{1,0:T(4,128)}, f32[3,32768]{1,0:T(4,128)}, u32[]{:S(2)}, u32[]{:S(2)}) %collective-permute-start.2) | collective-permute-done | bytes 393248 | tf_op jit(solution)/shard_map/ppermute | solution.py:360
  15.9 1.4 %fusion.grads_ref = f32[256,8,128]{2,1,0:T(8,128)S(1)} fusion(f32[3,256,128]{2,0,1:T(4,128)} %bitcast.3, f32[3,256,128]{2,0,1:T(4,128)} %bitcast.24), kind=kLoop, calls=%fused_computation.2 | loop fusion | flops 1310720 | bytes 1835008 | tf_op jit(solution)/shard_map/transpose | solution.py:369
  17.3 30.3 %load_terms.1.load_ref = f32[264,8,128]{2,1,0:T(8,128)S(1)} custom-call(s32[2048]{0:T(1024)S(1)} %sub.34.lists_ref, s32[256]{0:T(256)S(1)} %get-tuple-element.7.order_ref, s32[9]{0:T(128)S(1)} %pad_add_fusion.trips_ref, f32[256,8,128]{2,1,0:T(8,128)S(1)} %fusion.grads_ref, f32[256,8,128]{2,1,0:T(8,128)S(1)} %pad.30.points_ref, f32[512,8,128]{2,1,0:T(8,128)S(1)} %pad.31.ctrl_ref), custom_call_target="tpu_custom_call" | custom-call | tf_op jit(solution)/shard_map/load_terms/pallas_call | solution.py:388
  47.6 41.5 %scatter_and_solve.1 = (f32[32,4,128]{2,1,0:T(4,128)S(1)}, f32[32,4,128]{2,1,0:T(4,128)S(1)}) custom-call(f32[288]{0:T(512)S(1)} %reshape.111.mask_ref, f32[264,8,128]{2,1,0:T(8,128)S(1)} %load_terms.1.load_ref, f32[40,8,128]{2,1,0:T(8,128)S(1)} %pad_dynamic-slice_fusion.points_ref), custom_call_target="tpu_custom_call" | custom-call | tf_op jit(solution)/shard_map/scatter_and_solve/pallas_call | solution.py:401
  89.2 0.7 slice_bitcast_fusion
  (12 shorter events, 0.2 us)
Async XLA Ops:
  0.6 15.3 %collective-permute-start.2 = (f32[3,32768]{1,0:T(4,128)}, f32[3,32768]{1,0:T(4,128)}, u32[]{:S(2)}, u32[]{:S(2)}) collective-permute-start(f32[3,32768]{1,0:T(4,128)} %param.7), channel_id=1, source_target_pairs={{0,16},{16,0},{1,17},{17,1},{2,18},{18,2},{3,19},{19,3},{4,20},{20... | collective-permute-start | bytes 1179656 | tf_op jit(solution)/shard_map/ppermute | solution.py:360
  4.6 8.8 %collective-permute-start = (f32[2,8]{0,1:T(8,128)S(1)}, f32[2,8]{0,1:T(8,128)S(1)}, u32[]{:S(2)}, u32[]{:S(2)}) collective-permute-start(f32[2,8]{0,1:T(8,128)S(1)} %get-tuple-element.13), channel_id=1, source_target_pairs={{0,1},{1,2},{2,3},{3,4},{4,5},{5,6},{6,7},{7,8},{8,9},{9,10},{10,1... | collective-permute-start | bytes 200 | tf_op jit(solution)/shard_map/ppermute | solution.py:331
  6.1 7.3 %collective-permute-start.1 = (f32[2,8]{0,1:T(8,128)S(1)}, f32[2,8]{0,1:T(8,128)S(1)}, u32[]{:S(2)}, u32[]{:S(2)}) collective-permute-start(f32[2,8]{0,1:T(8,128)S(1)} %get-tuple-element.14), channel_id=1, source_target_pairs={{1,0},{2,1},{3,2},{4,3},{5,4},{6,5},{7,6},{8,7},{9,8},{10,9},{11,1... | collective-permute-start | bytes 200 | tf_op jit(solution)/shard_map/ppermute | solution.py:332
  12.1 1.0 %copy-start = (f32[3,32768]{1,0:T(4,128)S(1)}, f32[3,32768]{1,0:T(4,128)}, u32[]{:S(2)}) copy-start(f32[3,32768]{1,0:T(4,128)} %param.6) | copy-start | bytes 1179652

commit v3 on v2

--- a/solution.py
+++ b/solution.py
@@ -104,8 +104,8 @@
 
 def solve_kernel(
     vols, ctrls, shared, mask_ref, load_ref, points_ref, sol_ref, res_ref,
-    from_pair, to_chip, from_chip, gathered, to_case, parts, cols, kern, field, first_w, second_w, start_w, sums_a, sums_b,
-    pair_send, pair_recv, chip_send, chip_recv, a_send, a_recv, b_send, b_recv, case_send, case_recv,
+    from_pair, to_chip, from_chip, gathered, to_case, parts, away, cols, kern, field, first_w, second_w, start_w, sums_a, sums_b,
+    pair_send, pair_recv, chip_send, chip_recv, a_send, a_recv, b_send, b_recv, case_send, case_recv, edge_send, edge_recv,
 ):
     count = vols * ctrls
     chips = count // 2
@@ -157,6 +157,20 @@
             device_id_type=MESH,
         )
 
+    def edge_copy(side):
+        return pltpu.make_async_remote_copy(
+            src_ref=mask_ref.at[pl.ds((0, own - 2)[side], 2)],
+            dst_ref=away.at[pl.ds((own + 2, 0)[side], 2)],
+            send_sem=edge_send.at[side],
+            recv_sem=edge_recv.at[side],
+            device_id=device((me + (count - 1, 1)[side]) % count),
+            device_id_type=MESH,
+        )
+
+    for side in range(2):
+        edge_copy(side).start()
+    away[2 : 2 + own] = mask_ref[...]
+
     def start_pair(step, _):
         pair_copy((chip + step) % chips).start()
         return 0
@@ -180,11 +194,13 @@
 
     lax.fori_loop(0, wide, turn, 0)
 
+    for side in range(2):
+        edge_copy(side).wait()
+
     def build(row, _):
         for entry in range(KN):
-            away = 1e6 * (1.0 - mask_ref[row * 8 + entry])
             kern[row, entry * 256 : entry * 256 + 256, :] = phi_tile(
-                column_reader(cols, row + entry), points_ref[row + 2] + away
+                column_reader(cols, row + entry), points_ref[row + 2] + away[row, entry : entry + 1, :]
             )
         return 0
 
@@ -219,20 +235,19 @@
         start_w[...] = gathered[:, 0:4]
 
     def spread(source, size):
-        def body(row, _):
-            parts = split_rows(source[row])
-            field[row] = jnp.concatenate([parts, jnp.zeros_like(parts)], axis=0).astype(jnp.bfloat16)
-            return 0
-
-        lax.fori_loop(0, size, body, 0)
+        value = source[0:size]
+        lead = value.astype(jnp.bfloat16).astype(jnp.float32)
+        blank = jnp.zeros((size, 8, TILE), jnp.float32)
+        field[0:size] = jnp.concatenate([lead, value - lead, blank], axis=1).astype(jnp.bfloat16)
 
     def apply(source, target, size, shift):
         spread(source, size + 4)
+        many = next(k for k in (12, 8, 4) if size % k == 0)
 
         def body(step, _):
             mixed = []
-            for turn in range(4):
-                row = step * 4 + turn
+            for turn in range(many):
+                row = step * many + turn
                 pieces = []
                 for entry in range(KN):
                     pieces += [field[row + entry]] * 2
@@ -243,12 +258,12 @@
                         preferred_element_type=jnp.float32,
                     )
                 )
-            for turn in range(4):
-                row = step * 4 + turn
+            for turn in range(many):
+                row = step * many + turn
                 target[row] = source[row + 2] + kernel_weight / 256.0 * (mixed[turn][0:4] + mixed[turn][4:8])
             return 0
 
-        lax.fori_loop(0, size // 4, body, 0)
+        lax.fori_loop(0, size // many, body, 0)
 
     def share(sums, send, recv):
         def copy(peer, slot):
@@ -325,14 +340,6 @@
     finish_b()
 
 
-def with_neighbours(rows, axes):
-    count = lax.axis_size(axes)
-    pairs = [(i, i + 1) for i in range(count - 1)]
-    before = lax.ppermute(rows[-2:], axes, pairs)
-    after = lax.ppermute(rows[:2], axes, [(j, i) for i, j in pairs])
-    return jnp.concatenate([before, rows, after], axis=0)
-
-
 def body(vols, ctrls, ctrl_coords, vol_coords, sensitivity, vol_lists, ctrl_lists):
     f32 = jnp.float32
     axes = ("vol", "ctrl")
@@ -346,7 +353,8 @@
     ids = first + jnp.arange(own, dtype=jnp.int32)
     wanted = ids[:, None] + jnp.arange(-2, 3, dtype=jnp.int32)
     listed = jnp.any(ctrl_lists[:, :, None] == wanted[:, None, :], axis=1) & (wanted >= 0)
-    mask = with_neighbours(jnp.pad(listed.astype(f32), ((0, 0), (0, 3))), axes).reshape(-1)
+    mask = jnp.pad(jnp.where(listed, 0.0, 1e6).astype(f32), ((0, 0), (0, 3)))
+    mask = jnp.broadcast_to(mask[:, :, None], (own, 8, TILE))
 
     doubles = (2.0 * ctrl_coords).reshape(3, tiles, TILE).transpose(1, 0, 2)
     ctrl_pack = jnp.pad(doubles, ((0, 0), (4, 1), (0, 0)))
@@ -401,7 +409,7 @@
     sol, res = pl.pallas_call(
         functools.partial(solve_kernel, vols, ctrls, shared),
         out_shape=(answer, answer),
-        in_specs=[smem, vmem, vmem],
+        in_specs=[vmem, vmem, vmem],
         out_specs=(vmem, vmem),
         scratch_shapes=[
             pltpu.VMEM((chips, width, 8, TILE), f32),
@@ -410,6 +418,7 @@
             pltpu.VMEM((width, 8, TILE), f32),
             pltpu.VMEM((width, 4, TILE), f32),
             pltpu.VMEM((2, width, 4, TILE), f32),
+            pltpu.VMEM((own + 4, 8, TILE), f32),
             pltpu.VMEM((wide, 3, TILE, TILE), f32),
             pltpu.VMEM((own + 4, KN * 256, TILE), jnp.bfloat16),
             pltpu.VMEM((wide, 16, TILE), jnp.bfloat16),
@@ -419,7 +428,7 @@
             pltpu.VMEM((count, 8, TILE), f32),
             pltpu.VMEM((count, 16, TILE), f32),
             dma((chips,)), dma((chips,)), dma((chips,)), dma((chips,)),
-            dma((count,)), dma((count,)), dma((count,)), dma((count,)), dma((1,)), dma((1,)),
+            dma((count,)), dma((count,)), dma((count,)), dma((count,)), dma((1,)), dma((1,)), dma((2,)), dma((2,)),
         ],
         compiler_params=pltpu.CompilerParams(
             collective_id=0, has_side_effects=True, vmem_limit_bytes=40 * 2**20

time: 89.7 us -> 90 us (level)
  waiting for transfers between devices: 2.24 us -> 6.32 us
  starting transfers between devices: 5.77 us -> 3.03 us
  Pallas kernels: 71.8 us -> 72.8 us
  other arithmetic: 5.55 us -> 4.62 us
    ppermute x1, waiting for transfers between devices: 2.24 us -> 6.32 us  [body(): other = lax.ppermute(sensitivity, 'cases', [(0, 1), (1, 0)])]
    ppermute x2 -> x0, starting transfers between devices: 2.74 us -> none  [the longest x1 1.45 us: with_neighbours(): before = lax.ppermute(rows[-2:], axes, pairs)]
    pallas_call x1, Pallas kernels: 41.5 us -> 42.5 us  [body(): pl.pallas_call(functools.partial(solve_kernel, vols, ctrls, shared), out_...]
  transfers between devices with their start and end apart: 3 -> 1, of which waited for: 1 -> 1; matrix products, arithmetic and copies ran while one was open for 6% -> 5% of each run, Pallas kernels for 0% -> 0%
where the time goes in v3:
time: 90 us; the launch traced here: 90.7 us
  Pallas kernels  72.8 us (81%)
  waiting for transfers between devices  6.32 us (7%)
  other arithmetic  4.62 us (5%)
  starting transfers between devices  3.03 us (3%)
  local copies, waits for them, and re-layouts  2.56 us (3%)
  between operations  1.44 us (2%)
    pallas_call x1, Pallas kernels, body(): pl.pallas_call(functools.partial(solve_kernel, vols, ctrls, shared), out_...  42.5 us
    pallas_call x1, Pallas kernels, body(): pl.pallas_call(functools.partial(load_kernel, own, half), out_shape=jax.S...  30.2 us
    ppermute x1, waiting for transfers between devices, body(): other = lax.ppermute(sensitivity, 'cases', [(0, 1), (1, 0)])  6.32 us
    ppermute x1, starting transfers between devices, body(): other = lax.ppermute(sensitivity, 'cases', [(0, 1), (1, 0)])  3.03 us
  transfers between devices with their start and end apart: 1, of which 1 were waited for; matrix products, arithmetic and copies ran while one was open for 5% of the time, Pallas kernels for 0%

profile of v3, /device:TPU:0, one launch (start us, length us, event | category | flops | bytes accessed | tf_op | source)
XLA Modules:
  0.0 90.7 jit_solution(4429924527041320574)
XLA Ops:
  0.6 0.0 copy-start
  0.6 3.0 %collective-permute-start = (f32[3,32768]{1,0:T(4,128)}, f32[3,32768]{1,0:T(4,128)}, u32[]{:S(2)}, u32[]{:S(2)}) collective-permute-start(f32[3,32768]{1,0:T(4,128)} %param.7), channel_id=1, source_target_pairs={{0,16},{16,0},{1,17},{17,1},{2,18},{18,2},{3,19},{19,3},{4,20},{20... | collective-permute-start | bytes 1179656 | tf_op jit(solution)/shard_map/ppermute | solution.py:368
  3.7 0.7 convert_reduce_fusion
  4.4 0.3 reduce-window.9
  4.7 0.1 slice.16
  4.9 0.1 slice_reduce_fusion
  5.0 0.1 add_bitcast_fusion
  5.0 0.6 slice.18
  5.6 0.2 select_reduce_fusion
  5.8 0.1 reshape.110
  5.9 0.1 reduce_sum.49
  6.1 0.1 copy.16
  6.2 0.1 sub.34.lists_ref
  6.3 1.5 %multiply_bitcast_fusion = f32[512,3,128]{2,1,0:T(4,128)S(1)} fusion(f32[3,65536]{1,0:T(4,128)} %param.5), kind=kLoop, calls=%fused_computation.5 | loop fusion | flops 196608 | bytes 1572864 | tf_op jit(solution)/shard_map/transpose | solution.py:359
  7.8 0.0 copy-done
  7.8 0.1 multiply_bitcast_fusion.1
  7.9 0.0 copy-start.2
  7.9 0.2 pad.27.ctrl_ref
  8.2 0.1 pad.26.points_ref
  8.3 0.1 broadcast_add_fusion.3
  8.3 0.3 copy-done.2
  8.6 0.1 and_select_fusion
  8.7 0.1 copy.17
  9.5 0.0 copy-start.1
  9.5 0.1 pad_add_fusion.trips_ref
  9.6 6.3 %collective-permute-done = f32[3,32768]{1,0:T(4,128)} collective-permute-done((f32[3,32768]{1,0:T(4,128)}, f32[3,32768]{1,0:T(4,128)}, u32[]{:S(2)}, u32[]{:S(2)}) %collective-permute-start) | collective-permute-done | bytes 393248 | tf_op jit(solution)/shard_map/ppermute | solution.py:368
  15.9 0.0 copy-done.1
  15.9 1.3 %fusion.grads_ref = f32[256,8,128]{2,1,0:T(8,128)S(1)} fusion(f32[3,256,128]{2,0,1:T(4,128)} %bitcast.3, f32[3,256,128]{2,0,1:T(4,128)S(1)} %bitcast.24), kind=kLoop, calls=%fused_computation.2 | loop fusion | flops 1310720 | bytes 1835008 | tf_op jit(solution)/shard_map/transpose | solution.py:377
  17.2 30.2 %load_terms.1.load_ref = f32[264,8,128]{2,1,0:T(8,128)S(1)} custom-call(s32[2048]{0:T(1024)S(1)} %sub.34.lists_ref, s32[256]{0:T(256)S(1)} %get-tuple-element.7.order_ref, s32[9]{0:T(128)S(1)} %pad_add_fusion.trips_ref, f32[256,8,128]{2,1,0:T(8,128)S(1)} %fusion.grads_ref, f32[256,8,128]{2,1,0:T(8,128)S(1)} %pad.26.points_ref, f32[512,8,128]{2,1,0:T(8,128)S(1)} %pad.27.ctrl_ref), custom_call_target="tpu_custom_call" | custom-call | tf_op jit(solution)/shard_map/load_terms/pallas_call | solution.py:396
  47.5 0.1 broadcast_in_dim.62.mask_ref
  47.5 42.5 %scatter_and_solve.1 = (f32[32,4,128]{2,1,0:T(4,128)S(1)}, f32[32,4,128]{2,1,0:T(4,128)S(1)}) custom-call(f32[32,8,128]{2,1,0:T(8,128)S(1)} %broadcast_in_dim.62.mask_ref, f32[264,8,128]{2,1,0:T(8,128)S(1)} %load_terms.1.load_ref, f32[40,8,128]{2,1,0:T(8,128)S(1)} %pad_dynamic-slice_fusion.points_ref), custom_call_target="tpu_custom_call" | custom-call | tf_op jit(solution)/shard_map/scatter_and_solve/pallas_call | solution.py:409
  90.1 0.7 slice_bitcast_fusion
  (13 shorter events, 0.2 us)
Async XLA Ops:
  0.6 7.2 %copy-start = (f32[3,32768]{1,0:T(4,128)S(1)}, f32[3,32768]{1,0:T(4,128)}, u32[]{:S(2)}) copy-start(f32[3,32768]{1,0:T(4,128)} %param.6) | copy-start | bytes 1179652
  0.6 15.3 %collective-permute-start = (f32[3,32768]{1,0:T(4,128)}, f32[3,32768]{1,0:T(4,128)}, u32[]{:S(2)}, u32[]{:S(2)}) collective-permute-start(f32[3,32768]{1,0:T(4,128)} %param.7), channel_id=1, source_target_pairs={{0,16},{16,0},{1,17},{17,1},{2,18},{18,2},{3,19},{19,3},{4,20},{20... | collective-permute-start | bytes 1179656 | tf_op jit(solution)/shard_map/ppermute | solution.py:368
  7.9 0.7 copy-start.2
  9.5 6.5 %copy-start.1 = (f32[3,32768]{1,0:T(4,128)S(1)}, f32[3,32768]{1,0:T(4,128)}, u32[]{:S(2)}) copy-start(f32[3,32768]{1,0:T(4,128)} %param.7) | copy-start | bytes 1179652

commit v4 on v3

--- a/solution.py
+++ b/solution.py
@@ -192,7 +192,7 @@
         turn_columns(cols, row, points_ref[row])
         return 0
 
-    lax.fori_loop(0, wide, turn, 0)
+    lax.fori_loop(0, KN, turn, 0)
 
     for side in range(2):
         edge_copy(side).wait()
@@ -202,7 +202,7 @@
             kern[row, entry * 256 : entry * 256 + 256, :] = phi_tile(
                 column_reader(cols, row + entry), points_ref[row + 2] + away[row, entry : entry + 1, :]
             )
-        return 0
+        return turn(jnp.minimum(row + KN, wide - 1), 0)
 
     lax.fori_loop(0, own + HALO, build, 0)
 

time: 90 us -> 88.8 us (0.987)
  Pallas kernels: 72.8 us -> 70.7 us
    pallas_call x1, Pallas kernels: 42.5 us -> 40.4 us  [body(): pl.pallas_call(functools.partial(solve_kernel, vols, ctrls, shared), out_...]
where the time goes in v4:
time: 88.8 us; the launch traced here: 88.7 us
  Pallas kernels  70.7 us (80%)
  waiting for transfers between devices  6.32 us (7%)
  other arithmetic  4.62 us (5%)
  starting transfers between devices  3.03 us (3%)
  local copies, waits for them, and re-layouts  2.56 us (3%)
  between operations  1.44 us (2%)
    pallas_call x1, Pallas kernels, body(): pl.pallas_call(functools.partial(solve_kernel, vols, ctrls, shared), out_...  40.4 us
    pallas_call x1, Pallas kernels, body(): pl.pallas_call(functools.partial(load_kernel, own, half), out_shape=jax.S...  30.3 us
    ppermute x1, waiting for transfers between devices, body(): other = lax.ppermute(sensitivity, 'cases', [(0, 1), (1, 0)])  6.32 us
    ppermute x1, starting transfers between devices, body(): other = lax.ppermute(sensitivity, 'cases', [(0, 1), (1, 0)])  3.03 us
  transfers between devices with their start and end apart: 1, of which 1 were waited for; matrix products, arithmetic and copies ran while one was open for 5% of the time, Pallas kernels for 0%

profile of v4, /device:TPU:0, one launch (start us, length us, event | category | flops | bytes accessed | tf_op | source)
XLA Modules:
  0.0 88.7 jit_solution(1287430689007841847)
XLA Ops:
  0.6 0.0 copy-start
  0.6 3.0 %collective-permute-start = (f32[3,32768]{1,0:T(4,128)}, f32[3,32768]{1,0:T(4,128)}, u32[]{:S(2)}, u32[]{:S(2)}) collective-permute-start(f32[3,32768]{1,0:T(4,128)} %param.7), channel_id=1, source_target_pairs={{0,16},{16,0},{1,17},{17,1},{2,18},{18,2},{3,19},{19,3},{4,20},{20... | collective-permute-start | bytes 1179656 | tf_op jit(solution)/shard_map/ppermute | solution.py:368
  3.7 0.7 convert_reduce_fusion
  4.4 0.3 reduce-window.9
  4.7 0.1 slice.16
  4.9 0.1 slice_reduce_fusion
  5.0 0.1 add_bitcast_fusion
  5.0 0.6 slice.18
  5.6 0.2 select_reduce_fusion
  5.8 0.1 reshape.110
  5.9 0.1 reduce_sum.49
  6.1 0.1 copy.16
  6.2 0.1 sub.34.lists_ref
  6.3 1.5 %multiply_bitcast_fusion = f32[512,3,128]{2,1,0:T(4,128)S(1)} fusion(f32[3,65536]{1,0:T(4,128)} %param.5), kind=kLoop, calls=%fused_computation.5 | loop fusion | flops 196608 | bytes 1572864 | tf_op jit(solution)/shard_map/transpose | solution.py:359
  7.8 0.0 copy-done
  7.8 0.1 multiply_bitcast_fusion.1
  7.9 0.0 copy-start.2
  7.9 0.2 pad.27.ctrl_ref
  8.2 0.1 pad.26.points_ref
  8.3 0.1 broadcast_add_fusion.3
  8.3 0.3 copy-done.2
  8.6 0.1 and_select_fusion
  8.7 0.1 copy.17
  9.5 0.0 copy-start.1
  9.5 0.1 pad_add_fusion.trips_ref
  9.6 6.3 %collective-permute-done = f32[3,32768]{1,0:T(4,128)} collective-permute-done((f32[3,32768]{1,0:T(4,128)}, f32[3,32768]{1,0:T(4,128)}, u32[]{:S(2)}, u32[]{:S(2)}) %collective-permute-start) | collective-permute-done | bytes 393248 | tf_op jit(solution)/shard_map/ppermute | solution.py:368
  15.9 0.0 copy-done.1
  15.9 1.3 %fusion.grads_ref = f32[256,8,128]{2,1,0:T(8,128)S(1)} fusion(f32[3,256,128]{2,0,1:T(4,128)} %bitcast.3, f32[3,256,128]{2,0,1:T(4,128)S(1)} %bitcast.24), kind=kLoop, calls=%fused_computation.2 | loop fusion | flops 1310720 | bytes 1835008 | tf_op jit(solution)/shard_map/transpose | solution.py:377
  17.2 30.3 %load_terms.1.load_ref = f32[264,8,128]{2,1,0:T(8,128)S(1)} custom-call(s32[2048]{0:T(1024)S(1)} %sub.34.lists_ref, s32[256]{0:T(256)S(1)} %get-tuple-element.7.order_ref, s32[9]{0:T(128)S(1)} %pad_add_fusion.trips_ref, f32[256,8,128]{2,1,0:T(8,128)S(1)} %fusion.grads_ref, f32[256,8,128]{2,1,0:T(8,128)S(1)} %pad.26.points_ref, f32[512,8,128]{2,1,0:T(8,128)S(1)} %pad.27.ctrl_ref), custom_call_target="tpu_custom_call" | custom-call | tf_op jit(solution)/shard_map/load_terms/pallas_call | solution.py:396
  47.5 0.1 broadcast_in_dim.62.mask_ref
  47.6 40.4 %scatter_and_solve.1 = (f32[32,4,128]{2,1,0:T(4,128)S(1)}, f32[32,4,128]{2,1,0:T(4,128)S(1)}) custom-call(f32[32,8,128]{2,1,0:T(8,128)S(1)} %broadcast_in_dim.62.mask_ref, f32[264,8,128]{2,1,0:T(8,128)S(1)} %load_terms.1.load_ref, f32[40,8,128]{2,1,0:T(8,128)S(1)} %pad_dynamic-slice_fusion.points_ref), custom_call_target="tpu_custom_call" | custom-call | tf_op jit(solution)/shard_map/scatter_and_solve/pallas_call | solution.py:409
  88.0 0.7 slice_bitcast_fusion
  (13 shorter events, 0.2 us)
Async XLA Ops:
  0.6 7.2 %copy-start = (f32[3,32768]{1,0:T(4,128)S(1)}, f32[3,32768]{1,0:T(4,128)}, u32[]{:S(2)}) copy-start(f32[3,32768]{1,0:T(4,128)} %param.6) | copy-start | bytes 1179652
  0.6 15.3 %collective-permute-start = (f32[3,32768]{1,0:T(4,128)}, f32[3,32768]{1,0:T(4,128)}, u32[]{:S(2)}, u32[]{:S(2)}) collective-permute-start(f32[3,32768]{1,0:T(4,128)} %param.7), channel_id=1, source_target_pairs={{0,16},{16,0},{1,17},{17,1},{2,18},{18,2},{3,19},{19,3},{4,20},{20... | collective-permute-start | bytes 1179656 | tf_op jit(solution)/shard_map/ppermute | solution.py:368
  7.9 0.7 copy-start.2
  9.5 6.5 %copy-start.1 = (f32[3,32768]{1,0:T(4,128)S(1)}, f32[3,32768]{1,0:T(4,128)}, u32[]{:S(2)}) copy-start(f32[3,32768]{1,0:T(4,128)} %param.7) | copy-start | bytes 1179652
